TPU v7x, 1024 devices: a whole 8x8x8 slice. The times are simulated.
1024 devices in a mesh: node: 64 (over x, y), feat: 16 (over z, core).
Axes of the slice: x: 8, y: 8, z: 8, core: 2. Of those that a mesh axis runs over, the one named last changes fastest.
Arguments:
- features: bfloat16 [16384, 768], P('node', 'feat'), may hold values from -6 to 6
- weight: bfloat16 [768, 1024], P('feat'), may hold values from -0.3125 to 0.3125
- tile_weights: bfloat16 [128, 8, 128, 128], P('node'), may hold values from -0.1875 to 0.1875
- tile_cols: int32 [128, 8], P('node'), may hold values from 0 to 127, as said below
- tile_count: int32 [128], P('node'), may hold values from 1 to 8, as said below
- out_grad: bfloat16 [16384, 1024], P('node', 'feat'), may hold values from -6 to 6
- relu_mask: int32 [16384, 1024], P('node', 'feat'), may hold values 0 or 1
Outputs:
- activations: bfloat16 [16384, 1024], P('node', 'feat')
- feature_grad: bfloat16 [16384, 768], P('node', 'feat')
Inputs may be any that keep to these rules, and one draw needn't show every extreme that they name: `tile_cols`: the 8 column tiles of a row tile are distinct; the row tiles of one node block read at most 1 distinct column tiles of any one node block through used slots, and exactly 1 of some block in every node block. `tile_count`: every node block has a row tile with all 8 slots used.
All inputs are finite; a program needn't handle non-finite values. No bound on the sum of `relu_mask` on one device may be relied on, other than what follows from the above.
Results may differ from a plain program's by a relative error of at most 0.0049.
Values may be sent and summed in bfloat16 or wider, within the bound.
A program may use at most 32 MiB of HBM per device.

v0:
```python
import jax
import jax.numpy as jnp
from jax import lax
from jax.sharding import PartitionSpec as P

CAP = 1


def local(features, weight, tile_weights, tile_cols, tile_count, out_grad, relu_mask):
    count_blocks = lax.axis_size("node")
    rows_here = features.shape[0]
    tile_size = tile_weights.shape[2]
    tiles_here = tile_cols.shape[0]
    slot_total = tile_cols.shape[1]
    cols_here = weight.shape[1] // lax.axis_size("feat")
    refs_here = tiles_here * slot_total
    valid_ref = jnp.arange(slot_total, dtype=jnp.int32)[None, :] < tile_count[:, None]
    owner_block = tile_cols // tiles_here
    flat_cols = tile_cols.reshape(-1)
    flat_valid = valid_ref.reshape(-1)
    tile_ids = jnp.arange(count_blocks * tiles_here, dtype=jnp.int32)
    ref_hits = (flat_cols[:, None] == tile_ids[None, :]) & flat_valid[:, None]
    need_flags = jnp.any(ref_hits, axis=0).reshape(count_blocks, tiles_here)
    slot_rank = jnp.cumsum(need_flags.astype(jnp.int32), axis=1) - 1
    ref_slot = jnp.sum(jnp.where(ref_hits, slot_rank.reshape(1, -1), 0), axis=1)
    chosen_flags = need_flags[:, None, :] & (
        slot_rank[:, None, :] == jnp.arange(CAP, dtype=jnp.int32)[None, :, None]
    )
    request_list = (
        jnp.sum(
            jnp.where(chosen_flags, jnp.arange(tiles_here, dtype=jnp.int32)[None, None, :] + 1, 0),
            axis=2,
        )
        - 1
    )
    wanted_list = lax.all_to_all(request_list, "node", split_axis=0, concat_axis=0, tiled=True)
    ref_target = owner_block.reshape(-1) * CAP + ref_slot
    weight_part = weight
    mixed_cols = lax.psum_scatter(
        lax.dot_general(
            weight_part, features, (((0,), (1,)), ((), ())), preferred_element_type=jnp.float32
        ),
        "feat",
        scatter_dimension=0,
        tiled=True,
    ).astype(jnp.bfloat16)
    everything = lax.all_gather(mixed_cols, "node", axis=1, tiled=True)
    node_index = flat_cols[:, None] * tile_size + jnp.arange(tile_size, dtype=jnp.int32)[None, :]
    picked = jnp.take(everything, node_index.reshape(-1), axis=1).reshape(
        cols_here, tiles_here, slot_total, tile_size
    )
    source_here = picked.transpose(1, 2, 0, 3)
    source_here = jnp.where(valid_ref[:, :, None, None], source_here, jnp.zeros((), jnp.bfloat16))
    summed_rows = jnp.einsum(
        "tkcj,tkij->tic", source_here, tile_weights, preferred_element_type=jnp.float32
    )
    activations = jnp.maximum(summed_rows, 0.0).astype(jnp.bfloat16).reshape(rows_here, cols_here)
    masked_grad = (out_grad * relu_mask.astype(jnp.bfloat16)).reshape(
        tiles_here, tile_size, cols_here
    )
    reverse_terms = jnp.einsum(
        "tic,tkij->tkcj", masked_grad, tile_weights, preferred_element_type=jnp.float32
    )
    reverse_terms = jnp.where(valid_ref[:, :, None, None], reverse_terms, 0.0)
    outbound_sums = jax.ops.segment_sum(
        reverse_terms.reshape(refs_here, cols_here * tile_size),
        ref_target,
        num_segments=count_blocks * CAP,
    )
    outbound_sums = outbound_sums.reshape(count_blocks, CAP, cols_here, tile_size)
    inbound_sums = lax.all_to_all(outbound_sums, "node", split_axis=0, concat_axis=0, tiled=True)
    landing_ids = jnp.maximum(wanted_list.reshape(-1), 0)
    back_sums = jax.ops.segment_sum(
        inbound_sums.reshape(count_blocks * CAP, cols_here * tile_size),
        landing_ids,
        num_segments=tiles_here,
    )
    back_cols = (
        back_sums.reshape(tiles_here, cols_here, tile_size)
        .transpose(1, 0, 2)
        .reshape(cols_here, rows_here)
        .astype(jnp.bfloat16)
    )
    weight_part = weight
    grad_cols = jnp.dot(
        weight_part,
        lax.all_gather(back_cols, "feat", axis=0, tiled=True),
        preferred_element_type=jnp.float32,
    )
    feature_grad = grad_cols.T.astype(jnp.bfloat16)
    return (activations, feature_grad)


def solution(mesh):
    in_specs = (
        P("node", "feat"),
        P("feat", None),
        P("node", None, None, None),
        P("node", None),
        P("node"),
        P("node", "feat"),
        P("node", "feat"),
    )
    out_specs = (P("node", "feat"), P("node", "feat"))
    return jax.shard_map(local, mesh=mesh, in_specs=in_specs, out_specs=out_specs, check_vma=False)
```

profile of v0, /device:TPU:14, one launch (start us, length us, event | category | flops | bytes accessed | tf_op | source)
XLA Modules:
  0.0 200.5 jit_solution(12881783779014917560)
XLA Ops:
  7.2 0.0 copy-start
  7.2 0.0 copy-start.4
  7.2 0.0 copy-start.5
  7.2 0.0 copy-start.3
  7.2 0.0 copy-start.2
  7.2 0.0 reduce-scatter.2.cloned.1.call-start
  7.3 2.3 %fusion.28 = f32[1024,256]{1,0:T(8,128)} fusion(bf16[48,1024]{1,0:T(8,128)(2,1)} %param.8, bf16[256,48]{0,1:T(8,128)(2,1)} %param.7), kind=kOutput, calls=%fused_computation.57 | convolution fusion | flops 25165824 | bytes 1171456 | tf_op jit(solution)/shard_map/dot_general | solution.py:40
  9.5 0.0 reduce-scatter.2.cloned.1.call-update
  9.6 0.0 copy-done.4
  9.6 0.1 broadcast_in_dim_reshape.8
  9.6 0.0 copy-done.5
  9.6 0.1 iota_compare_fusion.1
  9.7 0.1 lt.53
  9.8 0.1 fusion.24
  9.9 0.1 broadcast_in_dim_reshape.9
  10.1 0.1 reshape.234
  10.2 0.2 reduce_window_sum.11
  10.4 0.1 select_reduce_fusion
  10.5 0.7 copy.39
  11.2 17.4 %all-to-all-start = ((s32[64,1,1]{2,1,0:T(1,128)}), s32[64,1,1]{2,1,0:T(1,128)S(1)}, u32[]{:S(2)}, u32[]{:S(2)}) async-start(s32[64,1,1]{2,1,0:T(1,128)} %copy.39), calls=%async_computation.1 | async-start | bytes 65536 | tf_op jit(solution)/shard_map/all_to_all | solution.py:36
  28.7 0.1 reshape.229
  28.7 0.1 sub.20
  28.9 0.0 copy-done.3
  28.9 0.0 copy-done.2
  28.9 0.2 select_reduce_fusion.1
  29.1 0.0 copy-done
  29.1 0.2 fusion.3
  29.4 2.0 scatter_custom_fusion
  31.4 1.7 copy.48
  33.1 4.9 %all-to-all-done = s32[64,1,1]{2,1,0:T(1,128)S(1)} async-done(((s32[64,1,1]{2,1,0:T(1,128)}), s32[64,1,1]{2,1,0:T(1,128)S(1)}, u32[]{:S(2)}, u32[]{:S(2)}) %all-to-all-start) | async-done | bytes 288 | tf_op jit(solution)/shard_map/all_to_all | solution.py:36
  38.0 7.8 %all-to-all-start.1 = ((f32[64,1,64,128]{3,2,1,0:T(8,128)}), f32[64,1,64,128]{3,2,1,0:T(8,128)S(1)}, u32[]{:S(2)}, u32[]{:S(2)}) async-start(f32[64,1,64,128]{3,2,1,0:T(8,128)} %bitcast.26), calls=%async_computation.2 | async-start | bytes 4194304 | tf_op jit(solution)/shard_map/all_to_all | solution.py:71
  45.8 0.0 copy-start.1
  45.8 0.2 all-gather.2.cloned.1.call-start
  46.1 42.2 %reduce-scatter.2.cloned.1.call-done = f32[64,256]{1,0:T(8,128)} async-done(((f32[1024,256]{1,0:T(8,128)}), f32[64,256]{1,0:T(8,128)}) %reduce-scatter.2.cloned.1.call-update) | async-done | bytes 65552 | tf_op jit(solution)/shard_map/reduce_scatter | solution.py:39
  88.2 1.5 convert_element_type.33
  89.7 0.0 all-gather.2.cloned.1.call-update
  89.7 0.1 fusion.22
  89.8 0.1 iota_add_fusion
  89.9 1.2 maximum_reduce_fusion
  91.1 1.9 all-to-all-done.1
  93.0 10.5 %scatter_custom_fusion.1 = f32[2,8192]{1,0:T(2,128)S(1)} fusion(s32[64]{0:T(128)S(1)} %maximum_reduce_fusion, f32[8,8,64,128]{3,2,1,0:T(8,128)S(1)} %bitcast.66, f32[]{:T(128)} %constant.47.clone.1), kind=kCustom, calls=%fused_computation.3 | custom fusion | flops 524288 | bytes 2162692 | tf_op jit(solution)/shard_map/scatter-add | solution.py:73
  103.6 31.0 %all_gather.7 = bf16[1024,256]{1,0:T(8,128)(2,1)S(1)} all-gather(bf16[64,256]{1,0:T(8,128)(2,1)S(1)} %bitcast.71), channel_id=1, replica_groups=mesh['node'=64,'feat'=16] {'feat'}, dimensions={0}, use_global_device_ids=true | all-gather | bytes 557056 | tf_op jit(solution)/shard_map/all_gather | solution.py:87
  134.6 0.0 copy-done.1
  134.6 0.8 convolution_convert_fusion
  135.4 44.0 %all-gather.2.cloned.1.call-done = bf16[64,16384]{1,0:T(8,128)(2,1)} async-done(((bf16[64,256]{1,0:T(8,128)(2,1)}), bf16[64,16384]{1,0:T(8,128)(2,1)}) %all-gather.2.cloned.1.call-update) | async-done | bytes 2097168 | tf_op jit(solution)/shard_map/all_gather | solution.py:47
  179.4 4.8 %copy.34 = bf16[64,16384]{0,1:T(8,128)(2,1)} copy(bf16[64,16384]{1,0:T(8,128)(2,1)} %all-gather.2.cloned.1.call-done) | data formatting | bytes 4194304 | tf_op jit(solution)/shard_map/all_gather | solution.py:47
  184.1 8.3 %gather_fusion = bf16[2048,64]{1,0:T(8,128)(2,1)S(1)} fusion(bf16[64,16384]{0,1:T(8,128)(2,1)} %copy.34, s32[2048]{0:T(1024)S(1)} %broadcast_clamp_fusion), kind=kCustom, calls=%fused_computation | custom fusion | bytes 532480 | tf_op jit(solution)/shard_map/jit(_take)/gather | solution.py:49
  192.5 0.2 copy.35
  192.7 0.3 fusion.6
  193.0 0.6 copy.64
  (13 shorter events, 0.1 us)
Async XLA Ops:
  7.2 22.0 %copy-start = (bf16[2,8,128,128]{3,2,1,0:T(8,128)(2,1)S(1)}, bf16[2,8,128,128]{3,2,1,0:T(8,128)(2,1)}, u32[]{:S(2)}) copy-start(bf16[2,8,128,128]{3,2,1,0:T(8,128)(2,1)} %param.9) | copy-start | bytes 1572868
  7.2 2.4 %copy-start.4 = (s32[2,8]{1,0:T(2,128)S(1)}, s32[2,8]{1,0:T(2,128)}, u32[]{:S(2)}) copy-start(s32[2,8]{1,0:T(2,128)} %param.10) | copy-start | bytes 196
  7.2 2.5 %copy-start.5 = (s32[2]{0:T(128)S(1)}, s32[2]{0:T(128)}, u32[]{:S(2)}) copy-start(s32[2]{0:T(128)} %param.11) | copy-start | bytes 28
  7.2 21.7 %copy-start.3 = (bf16[256,64]{0,1:T(8,128)(2,1)S(1)}, bf16[256,64]{0,1:T(8,128)(2,1)}, u32[]{:S(2)}) copy-start(bf16[256,64]{0,1:T(8,128)(2,1)} %param.12) | copy-start | bytes 98308
  7.2 21.7 %copy-start.2 = (s32[256,64]{0,1:T(8,128)S(1)}, s32[256,64]{0,1:T(8,128)}, u32[]{:S(2)}) copy-start(s32[256,64]{0,1:T(8,128)} %param.13) | copy-start | bytes 196612
  7.2 81.0 %reduce-scatter.2.cloned.1.call-start = ((), (), s32[]{:S(2)}) async-start(), calls=%async_computation.3 | async-start | bytes 1114112 | tf_op jit(solution)/shard_map/reduce_scatter | solution.py:39
  11.2 26.8 %all-to-all-start = ((s32[64,1,1]{2,1,0:T(1,128)}), s32[64,1,1]{2,1,0:T(1,128)S(1)}, u32[]{:S(2)}, u32[]{:S(2)}) async-start(s32[64,1,1]{2,1,0:T(1,128)} %copy.39), calls=%async_computation.1 | async-start | bytes 65536 | tf_op jit(solution)/shard_map/all_to_all | solution.py:36
  38.0 55.0 %all-to-all-start.1 = ((f32[64,1,64,128]{3,2,1,0:T(8,128)}), f32[64,1,64,128]{3,2,1,0:T(8,128)S(1)}, u32[]{:S(2)}, u32[]{:S(2)}) async-start(f32[64,1,64,128]{3,2,1,0:T(8,128)} %bitcast.26), calls=%async_computation.2 | async-start | bytes 4194304 | tf_op jit(solution)/shard_map/all_to_all | solution.py:71
  45.8 88.8 %copy-start.1 = (bf16[48,1024]{1,0:T(8,128)(2,1)S(1)}, bf16[48,1024]{1,0:T(8,128)(2,1)}, u32[]{:S(2)}) copy-start(bf16[48,1024]{1,0:T(8,128)(2,1)} %param.8) | copy-start | bytes 294916
  45.8 133.5 %all-gather.2.cloned.1.call-start = ((), (), s32[]{:S(2)}) async-start(), calls=%async_computation.4 | async-start | bytes 2129920 | tf_op jit(solution)/shard_map/all_gather | solution.py:47
Sparse Core Ops, SparseCore 0:
  11.4 76.7 reduce-scatter.1
  93.7 85.6 all-gather.1
where the time goes:
time: 201 us
  waiting for transfers between devices  93 us (46%)
  blocking collectives  31 us (15%)
  starting transfers between devices  25.5 us (13%)
  local copies, waits for them, and re-layouts  17.1 us (9%)
  other arithmetic  16 us (8%)
  between operations  14.3 us (7%)
  matrix products  3.64 us (2%)
    all_gather x1, waiting for transfers between devices, local(): everything = lax.all_gather(mixed_cols, 'node', axis=1, tiled=True)  44 us
    reduce_scatter x1, waiting for transfers between devices, local(): lax.psum_scatter(lax.dot_general(weight_part, features, (((0,), (1,)), ((...  42.2 us
    all_gather x1, blocking collectives, local(): lax.all_gather(back_cols, 'feat', axis=0, tiled=True)  31 us
    all_to_all x1, starting transfers between devices, local(): lax.all_to_all(request_list, 'node', split_axis=0, concat_axis=0, tiled=T...  17.4 us
    scatter-add x1, other arithmetic, local(): jax.ops.segment_sum(inbound_sums.reshape(count_blocks * CAP, cols_here *...  10.5 us
    gather x2, local copies, waits for them, and re-layouts, local(): jnp.take(everything, node_index.reshape(-1), axis=1)  8.53 us
    all_to_all x1, starting transfers between devices, local(): lax.all_to_all(outbound_sums, 'node', split_axis=0, concat_axis=0, tiled=...  7.8 us
    all_to_all x1, waiting for transfers between devices, local(): lax.all_to_all(request_list, 'node', split_axis=0, concat_axis=0, tiled=T...  4.9 us
  transfers between devices with their start and end apart: 4, of which 4 were waited for; matrix products, arithmetic and copies ran while one was open for 10% of the time, Pallas kernels for 0%

commit v1 on v0

v1 whole, which is shorter than its diff:
```python
import functools

import jax
import jax.numpy as jnp
from jax import lax
from jax.experimental import pallas as pl
from jax.experimental.pallas import tpu as pltpu
from jax.sharding import PartitionSpec as P

MESH = pl.DeviceIdType.MESH
R = 8
HALF = R // 2
U = 2
G = R // U
TILE = 128
UP, DOWN = 0, 1
STEP = (1, -1)
NEAR = (1, 7, 2, 6, 3, 5, 4)
NEAR_UNITS = (0, 3, 1, 2)
BF16, F32 = jnp.bfloat16, jnp.float32


def dot(a, b, dims=((1,), (0,))):
    return lax.dot_general(a, b, (dims, ((), ())), preferred_element_type=F32)


def kernel(
    source_ref, slot_ref, x_ref, w_ref, a_ref, g_ref, m_ref,
    act_ref, grad_ref,
    xall, first, parts, terms, kept, passed, landed, gall, zall, wall, wturn, outs,
    fs_recv, fh_recv, bh_recv, bs_recv, z_recv, sends,
):
    node, feat = lax.axis_index("node"), lax.axis_index("feat")
    x, y = node // R, lax.rem(node, R)
    z, core = feat // 2, lax.rem(feat, 2)
    din, dout = x_ref.shape[0], g_ref.shape[0]

    def on_first(t, d):
        if t == 0:
            return {"node": lax.rem(x + d + R, R) * R + y, "feat": feat}
        return {"node": x * R + lax.rem(y + d + R, R), "feat": feat}

    def on_ring(t, d):
        return on_first(1 - t, d)

    def on_z(d):
        return {"node": node, "feat": lax.rem(z + d, R) * 2 + core}

    partner = {"node": node, "feat": z * 2 + 1 - core}

    barrier = pltpu.get_barrier_semaphore()
    peers = [on_first(t, d) for t in (0, 1) for d in NEAR] + [on_z(d) for d in NEAR] + [partner]
    for peer in peers:
        pl.semaphore_signal(barrier, inc=1, device_id=peer, device_id_type=MESH)

    def place(t, e, d):
        return t * R * R + (e % R) * R + d % R

    def remote(src, dst, send_sem, recv_sem, to):
        return pltpu.make_async_remote_copy(
            src_ref=src, dst_ref=dst, send_sem=send_sem, recv_sem=recv_sem, device_id=to, device_id_type=MESH
        )

    def arrived(ref, sem):
        remote(ref, ref, sends.at[0], sem, partner).wait_recv()

    for t in (0, 1):
        xall[place(t, 0, 0)] = x_ref[:, t * TILE : (t + 1) * TILE]
    xall[2 * R * R] = jnp.zeros((din, TILE), BF16)
    for r in (0, 1):
        terms[r * 9 + 8] = jnp.zeros((din, TILE), F32)
    g_rows = lambda f: pl.ds(pl.multiple_of(f * dout, dout), dout)
    x_rows = lambda f: pl.ds(pl.multiple_of(f * din, din), din)
    gall[g_rows(feat), :] = g_ref[...] * m_ref[...].astype(BF16)
    columns = lambda zz: pl.ds(pl.multiple_of(zz * 2 * dout, 2 * dout), 2 * dout)
    wall[x_rows(feat), :] = w_ref[:, columns(z)]

    pl.semaphore_wait(barrier, len(peers))

    def z_start(k, buf, rows, source=None):
        for d in NEAR:
            src = buf.at[rows(feat), :] if source is None else source(lax.rem(z + d, R))
            remote(src, buf.at[rows(feat), :], sends.at[k], z_recv.at[k, feat], on_z(d)).start()
        remote(buf.at[rows(feat), :], buf.at[rows(feat), :], sends.at[k], z_recv.at[k, feat], partner).start()

    def z_forward(k, buf, rows):
        for d in NEAR:
            f = lax.rem(z - d + R, R) * 2 + core
            chunk = buf.at[rows(f), :]
            arrived(chunk, z_recv.at[k, f])
            remote(chunk, chunk, sends.at[k], z_recv.at[k, f], partner).start()

    def z_finish(k, buf, rows):
        for d in (0,) + NEAR:
            f = lax.rem(z - d + R, R) * 2 + 1 - core
            arrived(buf.at[rows(f), :], z_recv.at[k, f])

    def fs_start():
        for d in NEAR:
            for t in (0, 1):
                remote(
                    xall.at[place(t, 0, 0)], xall.at[place(t, 0, -d)], sends.at[3], fs_recv.at[t, -d % R], on_first(t, d)
                ).start()

    def fh_units(step, way):
        if step == HALF - 1:
            return [u for u in NEAR_UNITS if (u < G // 2) == (way == UP)]
        return NEAR_UNITS

    def fh_step(step):
        for place_at in range(G):
            for t in (0, 1):
                for way in (UP, DOWN):
                    units = fh_units(step, way)
                    if place_at >= len(units):
                        continue
                    u = units[place_at]
                    if step == 0 and way == UP:
                        for d in range(u * U, u * U + U):
                            if d:
                                arrived(xall.at[place(t, 0, d)], fs_recv.at[t, d])
                    chunk = xall.at[pl.ds(place(t, -STEP[way] * step, u * U), U)]
                    if step:
                        arrived(chunk, fh_recv.at[t, way, step - 1, u])
                    remote(
                        chunk,
                        xall.at[pl.ds(place(t, -STEP[way] * (step + 1), u * U), U)],
                        sends.at[3],
                        fh_recv.at[t, way, step, u],
                        on_ring(t, STEP[way]),
                    ).start()

    def fh_finish():
        for t in (0, 1):
            for way in (UP, DOWN):
                for step in (HALF - 2, HALF - 1):
                    for u in range(G):
                        if step == HALF - 2 and u in fh_units(HALF - 1, way):
                            continue
                        if step == HALF - 1 and u not in fh_units(step, way):
                            continue
                        chunk = xall.at[pl.ds(place(t, -STEP[way] * (step + 1), u * U), U)]
                        arrived(chunk, fh_recv.at[t, way, step, u])

    def aggregate():
        for r in (0, 1):
            total = jnp.zeros((din, TILE), F32)
            for k in range(8):
                total += dot(xall[source_ref[r, k]], a_ref[r, k], ((1,), (1,)))
            zall[x_rows(feat), r * TILE : (r + 1) * TILE] = total.astype(BF16)

    def finish_forward():
        result = dot(wturn[...], zall[...])
        outs[...] = jnp.maximum(result, 0.0)
        act_ref[...] = outs[pl.ds(pl.multiple_of(core * dout, dout), dout), :].astype(BF16)

    def make_terms():
        back = dot(w_ref[...], gall[...])
        high = back.astype(BF16)
        low = (back - high.astype(F32)).astype(BF16)
        both = jnp.concatenate([high, low], axis=0)
        for r in (0, 1):
            rows = both[:, r * TILE : (r + 1) * TILE]
            for k in range(8):
                term = dot(rows, a_ref[r, k])
                terms[r * 9 + k] = term[:din] + term[din:]

    def own(t, e, d):
        j = place(t, e, d)
        return terms[slot_ref[0, j]] + terms[slot_ref[1, j]]

    def part(t, way, step, u):
        return ((t * 2 + way) * HALF + step) * R + u * U

    def bh_units(step, way):
        if step == 0:
            return [u for u in range(G) if (u < G // 2) == (way == UP)]
        return range(G)

    def bh_step(step):
        for place_at in range(G):
            for t in (0, 1):
                for way in (UP, DOWN):
                    units = bh_units(step, way)
                    if place_at >= len(units):
                        continue
                    u = units[place_at]
                    e = STEP[way] * (HALF - step)
                    if step == 0:
                        ref, base = first, (t * G + u) * U
                    else:
                        ref, base = parts, part(t, way, step - 1, u)
                    coming = step > 1 or (step == 1 and u in bh_units(0, way))
                    chunk = ref.at[pl.ds(base, U)]
                    if coming:
                        arrived(chunk, bh_recv.at[t, way, step - 1, u])
                    for i in range(U):
                        value = own(t, e, u * U + i)
                        if coming:
                            value += ref[base + i].astype(F32)
                        ref[base + i] = value.astype(BF16)
                    remote(
                        chunk,
                        parts.at[pl.ds(part(t, way, step, u), U)],
                        sends.at[4],
                        bh_recv.at[t, way, step, u],
                        on_ring(t, STEP[way]),
                    ).start()

    def bs_start():
        for u in (0, 3, 1, 2):
            for t in (0, 1):
                for way in (UP, DOWN):
                    base = part(t, way, HALF - 1, u)
                    arrived(parts.at[pl.ds(base, U)], bh_recv.at[t, way, HALF - 1, u])
                for i in range(U):
                    d = u * U + i
                    value = own(t, 0, d)
                    for way in (UP, DOWN):
                        value += parts[part(t, way, HALF - 1, u) + i].astype(F32)
                    if d == 0:
                        kept[t] = value
                        continue
                    passed[t * R + d] = value.astype(BF16)
                    remote(
                        passed.at[t * R + d],
                        landed.at[t * R + (-d) % R],
                        sends.at[4],
                        bs_recv.at[t, -d % R],
                        on_first(t, d),
                    ).start()

    def bs_finish():
        for t in (0, 1):
            total = kept[t]
            for d in NEAR:
                arrived(landed.at[t * R + (-d) % R], bs_recv.at[t, -d % R])
                total += landed[t * R + (-d) % R].astype(F32)
            grad_ref[:, t * TILE : (t + 1) * TILE] = total.astype(BF16)

    fs_start()
    z_start(0, gall, g_rows)
    fh_step(0)
    z_start(1, wall, x_rows, lambda zz: w_ref.at[:, columns(zz)])
    fh_step(1)
    z_forward(0, gall, g_rows)
    fh_step(2)
    z_finish(0, gall, g_rows)
    fh_step(3)
    make_terms()
    bh_step(0)
    bh_step(1)
    fh_finish()
    aggregate()
    z_start(2, zall, x_rows)
    z_forward(1, wall, x_rows)
    bh_step(2)
    z_forward(2, zall, x_rows)
    bh_step(3)
    z_finish(1, wall, x_rows)
    wturn[...] = wall[...].T
    bs_start()
    z_finish(2, zall, x_rows)
    finish_forward()
    bs_finish()

    def left(ref, count, sem):
        for _ in range(count):
            remote(ref, ref, sem, z_recv.at[0, 0], partner).wait_send()

    z_bytes = [buf.at[pl.ds(0, (2 * R - 1) * rows), :] for buf, rows in ((gall, dout), (wall, din), (zall, din))]
    for k in range(3):
        left(z_bytes[k], 1, sends.at[k])
    left(xall.at[pl.ds(0, 2 * (R - 1) * (R + 1))], 1, sends.at[3])
    left(parts.at[pl.ds(0, 2 * (R - 1) * (R + 1))], 1, sends.at[4])


def local(features, weight, tile_weights, tile_cols, tile_count, out_grad, relu_mask):
    din, dout = features.shape[1], out_grad.shape[1]
    rows = features.shape[0]
    node = lax.axis_index("node")
    x, y = node // R, node % R
    block, t = tile_cols // 2, tile_cols % 2
    dx, dy = (block // R - x) % R, (block % R - y) % R
    where = jnp.where(t == 0, dy * R + dx, R * R + dx * R + dy)
    slots = jnp.arange(8, dtype=jnp.int32)[None, :]
    source = jnp.where(slots < tile_count[:, None], where, 2 * R * R).astype(jnp.int32)
    hits = source[:, :, None] == jnp.arange(2 * R * R, dtype=jnp.int32)[None, None, :]
    slot = jnp.sum(jnp.where(hits, slots[:, :, None] - 8, 0), axis=1) + 8
    slot = slot + 9 * jnp.arange(2, dtype=jnp.int32)[:, None]

    vmem = pl.BlockSpec(memory_space=pltpu.VMEM)
    smem = pl.BlockSpec(memory_space=pltpu.SMEM)
    dma = pltpu.SemaphoreType.DMA
    act, grad = pl.pallas_call(
        kernel,
        out_shape=(
            jax.ShapeDtypeStruct((dout, rows), BF16),
            jax.ShapeDtypeStruct((din, rows), BF16),
        ),
        in_specs=[smem, smem, vmem, vmem, vmem, vmem, vmem],
        out_specs=(vmem, vmem),
        scratch_shapes=[
            pltpu.VMEM((2 * R * R + 1, din, TILE), BF16),
            pltpu.VMEM((2 * R, din, TILE), BF16),
            pltpu.VMEM((4 * HALF * R, din, TILE), BF16),
            pltpu.VMEM((18, din, TILE), F32),
            pltpu.VMEM((2, din, TILE), F32),
            pltpu.VMEM((2 * R, din, TILE), BF16),
            pltpu.VMEM((2 * R, din, TILE), BF16),
            pltpu.VMEM((2 * R * dout, rows), BF16),
            pltpu.VMEM((2 * R * din, rows), BF16),
            pltpu.VMEM((2 * R * din, 2 * dout), BF16),
            pltpu.VMEM((2 * dout, 2 * R * din), BF16),
            pltpu.VMEM((2 * dout, rows), F32),
            dma((2, R)),
            dma((2, 2, HALF, G)),
            dma((2, 2, HALF, G)),
            dma((2, R)),
            dma((3, 2 * R)),
            dma((5,)),
        ],
        compiler_params=pltpu.CompilerParams(
            collective_id=0, has_side_effects=True, vmem_limit_bytes=24 * 1024 * 1024
        ),
        name="graph_layer",
    )(source, slot, features.T, weight, tile_weights, out_grad.T, relu_mask.T)
    return act.T, grad.T


def solution(mesh):
    in_specs = (
        P("node", "feat"),
        P("feat", None),
        P("node", None, None, None),
        P("node", None),
        P("node"),
        P("node", "feat"),
        P("node", "feat"),
    )
    out_specs = (P("node", "feat"), P("node", "feat"))
    return jax.shard_map(local, mesh=mesh, in_specs=in_specs, out_specs=out_specs, check_vma=False)
```

time: 201 us -> 66.3 us (0.33)
  waiting for transfers between devices: 93 us -> 0 us
  Pallas kernels: 0 us -> 59.7 us
  blocking collectives: 31 us -> 0 us
  starting transfers between devices: 25.5 us -> 0 us
  other arithmetic: 16 us -> 0.24 us
  between operations: 14.3 us -> 0.7 us
  local copies, waits for them, and re-layouts: 17.1 us -> 4.65 us
  matrix products: 3.64 us -> 0 us
    pallas_call x0 -> x1, Pallas kernels: none -> 59.7 us  [local(): pl.pallas_call(kernel, out_shape=(jax.ShapeDtypeStruct((dout, rows), BF16...]
    all_gather x1 -> x0, waiting for transfers between devices: 44 us -> none  [local(): everything = lax.all_gather(mixed_cols, 'node', axis=1, tiled=True)]
    reduce_scatter x1 -> x0, waiting for transfers between devices: 42.2 us -> none  [local(): lax.psum_scatter(lax.dot_general(weight_part, features, (((0,), (1,)), ((...]
    all_gather x1 -> x0, blocking collectives: 31 us -> none  [local(): lax.all_gather(back_cols, 'feat', axis=0, tiled=True)]
    all_to_all x2 -> x0, starting transfers between devices: 25.2 us -> none  [the longest x1 17.4 us: local(): lax.all_to_all(request_list, 'node', split_axis=0, concat_axis=0, tiled=T...]
    scatter-add x2 -> x0, other arithmetic: 12.5 us -> none  [the longest x1 10.5 us: local(): jax.ops.segment_sum(inbound_sums.reshape(count_blocks * CAP, cols_here *...]
    gather x2 -> x0, local copies, waits for them, and re-layouts: 8.53 us -> none  [local(): jnp.take(everything, node_index.reshape(-1), axis=1)]
    all_to_all x2 -> x0, waiting for transfers between devices: 6.79 us -> none  [the longest x1 4.9 us: local(): lax.all_to_all(request_list, 'node', split_axis=0, concat_axis=0, tiled=T...]
  transfers between devices with their start and end apart: 4 -> 0, of which waited for: 4 -> 0; matrix products, arithmetic and copies ran while one was open for 10% -> 0% of each run, Pallas kernels for 0% -> 0%
where the time goes in v1:
time: 66.3 us; the launch traced here: 65.3 us
  Pallas kernels  59.7 us (90%)
  local copies, waits for them, and re-layouts  4.65 us (7%)
  between operations  0.7 us (1%)
    pallas_call x1, Pallas kernels, local(): pl.pallas_call(kernel, out_shape=(jax.ShapeDtypeStruct((dout, rows), BF16...  59.7 us
    unnamed x16, local copies, waits for them, and re-layouts  4.65 us

profile of v1, /device:TPU:14, one launch (start us, length us, event | category | flops | bytes accessed | tf_op | source)
XLA Modules:
  0.0 65.3 jit_solution(8100048585820970829)
XLA Ops:
  0.6 0.0 copy-start.3
  0.6 0.0 copy-start.5
  0.7 0.0 copy-start.6
  0.7 0.0 copy-start.4
  0.7 0.6 copy-done.5
  1.3 0.0 copy-done.6
  1.3 0.1 compare_select_fusion.5.source_ref
  1.4 0.1 select_reduce_fusion
  1.5 0.1 add_add_fusion.slot_ref
  1.6 0.0 copy-done.3
  1.6 0.0 copy-done.4
  1.6 0.0 copy-start
  1.6 1.0 %copy-done = bf16[2,8,128,128]{3,2,1,0:T(8,128)(2,1)S(1)} copy-done((bf16[2,8,128,128]{3,2,1,0:T(8,128)(2,1)S(1)}, bf16[2,8,128,128]{3,2,1,0:T(8,128)(2,1)}, u32[]{:S(2)}) %copy-start) | copy-done | bytes 524312
  2.6 0.0 copy-start.1
  2.6 0.9 %copy-done.1 = bf16[48,1024]{1,0:T(8,128)(2,1)S(1)} copy-done((bf16[48,1024]{1,0:T(8,128)(2,1)S(1)}, bf16[48,1024]{1,0:T(8,128)(2,1)}, u32[]{:S(2)}) %copy-start.1) | copy-done | bytes 98328
  3.5 0.0 copy-start.2
  3.5 0.8 %copy-done.2 = s32[256,64]{0,1:T(8,128)S(1)} copy-done((s32[256,64]{0,1:T(8,128)S(1)}, s32[256,64]{0,1:T(8,128)}, u32[]{:S(2)}) %copy-start.2) | copy-done | bytes 65560
  4.4 59.7 %graph_layer.1 = (bf16[64,256]{1,0:T(8,128)(2,1)S(1)}, bf16[48,256]{1,0:T(8,128)(2,1)S(1)}) custom-call(s32[2,8]{1,0:T(2,128)S(1)} %compare_select_fusion.5.source_ref, s32[2,128]{1,0:T(2,128)S(1)} %add_add_fusion.slot_ref, bf16[48,256]{1,0:T(8,128)(2,1)S(1)} %bitcast.8, bf16[48,1024]{1,0:T(8,128)(2,1)S(1)} %copy-done.1, ...), custom_call_target="tpu_custom_call" | custom-call | tf_op jit(solution)/shard_map/graph_layer/pallas_call | solution.py:295
  64.1 0.6 copy.11
  64.7 0.6 copy.12
  (2 shorter events, 0.0 us)
Async XLA Ops:
  0.6 0.9 %copy-start.3 = (bf16[256,64]{0,1:T(8,128)(2,1)S(1)}, bf16[256,64]{0,1:T(8,128)(2,1)}, u32[]{:S(2)}) copy-start(bf16[256,64]{0,1:T(8,128)(2,1)} %param.12) | copy-start | bytes 98308
  0.6 0.7 %copy-start.5 = (s32[2,8]{1,0:T(2,128)S(1)}, s32[2,8]{1,0:T(2,128)}, u32[]{:S(2)}) copy-start(s32[2,8]{1,0:T(2,128)} %param.10) | copy-start | bytes 196
  0.7 0.7 %copy-start.6 = (s32[2]{0:T(128)S(1)}, s32[2]{0:T(128)}, u32[]{:S(2)}) copy-start(s32[2]{0:T(128)} %param.11) | copy-start | bytes 28
  0.7 0.9 %copy-start.4 = (bf16[256,48]{0,1:T(8,128)(2,1)S(1)}, bf16[256,48]{0,1:T(8,128)(2,1)}, u32[]{:S(2)}) copy-start(bf16[256,48]{0,1:T(8,128)(2,1)} %param.7) | copy-start | bytes 73732
  1.6 1.0 %copy-start = (bf16[2,8,128,128]{3,2,1,0:T(8,128)(2,1)S(1)}, bf16[2,8,128,128]{3,2,1,0:T(8,128)(2,1)}, u32[]{:S(2)}) copy-start(bf16[2,8,128,128]{3,2,1,0:T(8,128)(2,1)} %a_ref.1) | copy-start | bytes 1572868
  2.6 0.9 %copy-start.1 = (bf16[48,1024]{1,0:T(8,128)(2,1)S(1)}, bf16[48,1024]{1,0:T(8,128)(2,1)}, u32[]{:S(2)}) copy-start(bf16[48,1024]{1,0:T(8,128)(2,1)} %w_ref.1) | copy-start | bytes 294916
  3.5 0.8 %copy-start.2 = (s32[256,64]{0,1:T(8,128)S(1)}, s32[256,64]{0,1:T(8,128)}, u32[]{:S(2)}) copy-start(s32[256,64]{0,1:T(8,128)} %param.13) | copy-start | bytes 196612

commit v2 on v0

v2 whole, which is shorter than its diff:
```python
import jax
import jax.numpy as jnp
from jax import lax
from jax.experimental import pallas as pl
from jax.experimental.pallas import tpu as pltpu
from jax.sharding import PartitionSpec as P

MESH = pl.DeviceIdType.MESH
R = 8
TILE = 128
SLOTS = 8
BOTH = (0, 1)
OWN, OTHER = 0, 1
FAR = (4, 3, 5, 2, 6, 1, 7)
NEAR = FAR[::-1]
PER = R // 2
PART = PER // 2
SOURCES = ((1, 7, 3, 5), (0, 6, 2, 4))
LINES = 2 * R * PER
BF16, F32 = jnp.bfloat16, jnp.float32


def dot(a, b, dims=((1,), (0,))):
    return lax.dot_general(a, b, (dims, ((), ())), preferred_element_type=F32)


def back(axis, d):
    return (axis if d % 2 == 0 else 1 - axis), -d % R


def line(axis, d):
    return axis * R + d


def kernel(
    x_hbm, w_hbm, a_hbm, cols_hbm, count_hbm, g_hbm, m_hbm,
    act_ref, grad_ref,
    w_ref, a_ref, g_ref, m_ref, cols_ref, count_ref, table, slot_ref,
    asked, wanted, tiles, picked, got, terms, sent, back_in, kept, passed, landed, gall, zall, wall, wturn, outs,
    local_sem, q_recv, s_recv, h_recv, b_recv, l_recv, z_recv, w_recv, sends,
):
    node, feat = lax.axis_index("node"), lax.axis_index("feat")
    x, y = node // R, lax.rem(node, R)
    z, core = feat // 2, lax.rem(feat, 2)
    odd_block = lax.rem(x + y, 2)
    din, dout = x_hbm.shape[0], g_hbm.shape[0]

    def on_line(axis, d):
        along_x = lax.rem(x + d, R) * R + y
        along_y = x * R + lax.rem(y + d, R)
        use_y = odd_block if axis == OWN else 1 - odd_block
        return {"node": along_x + use_y * (along_y - along_x), "feat": feat}

    def on_z(d):
        return {"node": node, "feat": lax.rem(z + d + R, R) * 2 + core}

    partner = {"node": node, "feat": z * 2 + 1 - core}

    barrier = pltpu.get_barrier_semaphore()
    peers = [to for d in FAR for to in (on_line(OWN, d), on_line(OTHER, d), on_z(d))] + [partner]
    for peer in peers:
        pl.semaphore_signal(barrier, inc=1, device_id=peer, device_id_type=MESH)

    def fetch(src, dst, i):
        copy = pltpu.make_async_copy(src, dst, local_sem.at[i])
        copy.start()
        return copy

    get_cols, get_count = fetch(cols_hbm, cols_ref, 4), fetch(count_hbm, count_ref, 5)
    get_g, get_m = fetch(g_hbm, g_ref, 2), fetch(m_hbm, m_ref, 3)
    get_x = [fetch(x_hbm.at[:, pl.ds(t * TILE, TILE)], tiles.at[0, t], t) for t in BOTH]
    get_w, get_a = fetch(w_hbm, w_ref, 6), fetch(a_hbm, a_ref, 7)

    def remote(src, dst, send_sem, recv_sem, to):
        return pltpu.make_async_remote_copy(
            src_ref=src, dst_ref=dst, send_sem=send_sem, recv_sem=recv_sem, device_id=to, device_id_type=MESH
        )

    def arrived(ref, sem):
        remote(ref, ref, sends.at[0], sem, partner).wait_recv()

    g_rows = lambda f: pl.ds(pl.multiple_of(f * dout, dout), dout)
    x_rows = lambda f: pl.ds(pl.multiple_of(f * din, din), din)
    columns = lambda zz: pl.ds(pl.multiple_of(zz * 2 * dout, 2 * dout), 2 * dout)

    got[LINES] = jnp.zeros((din, TILE), BF16)
    for r in BOTH:
        terms[r * (SLOTS + 1) + SLOTS] = jnp.zeros((din, TILE), F32)

    get_cols.wait()
    get_count.wait()
    lanes = lax.broadcasted_iota(jnp.int32, (1, TILE), 1)
    rows = lax.broadcasted_iota(jnp.int32, asked.shape, 0)
    flags = jnp.zeros(asked.shape, jnp.int32)
    source = []
    for r in BOTH:
        row = jnp.full((1, TILE), r * (SLOTS + 1) + SLOTS, jnp.int32)
        for k in range(SLOTS):
            col = cols_ref[r, k]
            block = col >> 1
            bx, by = block >> 3, jnp.bitwise_and(block, R - 1)
            dx, dy = jnp.bitwise_and(bx - x + R, R - 1), jnp.bitwise_and(by - y + R, R - 1)
            odd = jnp.bitwise_and(bx + by, 1)
            d, i = jnp.where(odd == 1, dx, dy), jnp.where(odd == 1, dy, dx) >> 1
            i = jnp.where(i == 0, 0, jnp.where(i == 3, 1, i + 1))
            axis = jnp.where(odd == odd_block, OTHER, OWN)
            at = (axis * R + d) * PER + i
            used = k < count_ref[r]
            source.append(jnp.where(used, at, LINES))
            row = jnp.where(lanes == jnp.where(used, at, -1), r * (SLOTS + 1) + k, row)
            second = jnp.logical_and(used, jnp.bitwise_and(col, 1) == 1)
            flags = jnp.where(rows == jnp.where(second, (axis * R + d) * 8 + i, -1), 1, flags)
        table[r : r + 1, :] = row
    asked[...] = flags
    get_slot = fetch(table, slot_ref, 4)
    for axis in BOTH:
        mine = slice(line(axis, 0) * 8, line(axis, 0) * 8 + 8)
        wanted[mine, :] = flags[mine, :]
    get_g.wait()
    get_m.wait()
    gall[g_rows(feat), :] = g_ref[...] * m_ref[...].astype(BF16)
    get_w.wait()
    wall[x_rows(feat), :] = w_ref[:, columns(z)]
    for copy in get_x:
        copy.wait()

    pl.semaphore_wait(barrier, len(peers))

    def z_start(k, buf, rows):
        mine = buf.at[rows(feat), :]
        for to in [on_z(d) for d in FAR] + [partner]:
            remote(mine, mine, sends.at[k], z_recv.at[k, feat], to).start()

    def z_pass(k, buf, rows, distances):
        for d in distances:
            f = lax.rem(z + d, R) * 2 + core
            chunk = buf.at[rows(f), :]
            arrived(chunk, z_recv.at[k, f])
            remote(chunk, chunk, sends.at[k], z_recv.at[k, f], partner).start()

    def z_finish(k, buf, rows):
        for d in FAR + (0,):
            f = lax.rem(z + d, R) * 2 + 1 - core
            arrived(buf.at[rows(f), :], z_recv.at[k, f])

    def w_start():
        mine = x_rows(feat)
        for d in FAR:
            src = w_ref.at[:, columns(lax.rem(z + d, R))]
            remote(src, wall.at[mine, :], sends.at[2], w_recv.at[feat], on_z(d)).start()
        remote(wall.at[mine, :], wall.at[mine, :], sends.at[2], w_recv.at[feat], partner).start()

    def w_forward():
        for d in range(1, R):
            f = lax.rem(z + d, R) * 2 + core
            chunk = wall.at[x_rows(f), :]
            arrived(chunk, w_recv.at[f])
            remote(chunk, chunk, sends.at[2], w_recv.at[f], partner).start()

    def w_finish():
        for d in range(R):
            f = lax.rem(z + d, R) * 2 + 1 - core
            arrived(wall.at[x_rows(f), :], w_recv.at[f])
        wturn[...] = wall[...].T

    def ask():
        for d in FAR:
            for axis in BOTH:
                there, e = back(axis, d)
                remote(
                    asked.at[pl.ds(line(axis, d) * 8, 8), :],
                    wanted.at[pl.ds(line(there, e) * 8, 8), :],
                    sends.at[3],
                    q_recv.at[there, e],
                    on_line(axis, d),
                ).start()

    def spread():
        for d in FAR:
            remote(tiles.at[0], tiles.at[-d % R], sends.at[4], s_recv.at[-d % R], on_line(OWN, d)).start()

    def second_wanted(axis, d, i):
        row = line(axis, d) * 8 + i
        return wanted[row : row + 1, :] == 1

    def pick(axis, d, to, i):
        two = tiles[SOURCES[axis][i]].astype(F32)
        to[line(axis, d) * PER + i] = jnp.where(second_wanted(axis, d, i), two[1], two[0]).astype(BF16)

    def part(axis, d, half):
        return pl.ds(line(axis, d) * PER + half * PART, PART)

    def pass_on(half, order):
        blocks = range(half * PART, half * PART + PART)
        for axis in BOTH:
            for i in blocks:
                d = SOURCES[axis][i]
                if d:
                    arrived(tiles.at[d], s_recv.at[d])
        for d in order:
            for axis in BOTH:
                there, e = back(axis, d)
                if half == 0:
                    arrived(wanted.at[pl.ds(line(axis, d) * 8, 8), :], q_recv.at[axis, d])
                for i in blocks:
                    pick(axis, d, picked, i)
                remote(
                    picked.at[part(axis, d, half)],
                    got.at[part(there, e, half)],
                    sends.at[5],
                    h_recv.at[there, e, half],
                    on_line(axis, d),
                ).start()
        for axis in BOTH:
            for i in blocks:
                pick(axis, 0, got, i)

    def have_all():
        for half in BOTH:
            for axis in BOTH:
                for d in FAR:
                    arrived(got.at[part(axis, d, half)], h_recv.at[axis, d, half])

    def aggregate():
        for r in BOTH:
            total = jnp.zeros((din, TILE), F32)
            for k in range(SLOTS):
                total += dot(got[source[r * SLOTS + k]], a_ref[r, k], ((1,), (1,)))
            zall[x_rows(feat), r * TILE : (r + 1) * TILE] = total.astype(BF16)

    def finish_forward():
        outs[...] = jnp.maximum(dot(wturn[...], zall[...]), 0.0)
        act_ref[...] = outs[pl.ds(pl.multiple_of(core * dout, dout), dout), :].astype(BF16)

    def make_terms():
        back = dot(w_ref[...], gall[...])
        high = back.astype(BF16)
        low = (back - high.astype(F32)).astype(BF16)
        both = jnp.concatenate([high, low], axis=0)
        for r in BOTH:
            rows = both[:, r * TILE : (r + 1) * TILE]
            for k in range(SLOTS):
                term = dot(rows, a_ref[r, k])
                terms[r * (SLOTS + 1) + k] = term[:din] + term[din:]

    def own(axis, d, i):
        j = line(axis, d) * PER + i
        return terms[slot_ref[0, j]] + terms[slot_ref[1, j]]

    def send_terms(half):
        for d in FAR:
            for axis in BOTH:
                there, e = back(axis, d)
                for i in range(half * PART, half * PART + PART):
                    sent[line(axis, d) * PER + i] = own(axis, d, i).astype(BF16)
                remote(
                    sent.at[part(axis, d, half)],
                    back_in.at[part(there, e, half)],
                    sends.at[6],
                    b_recv.at[there, e, half],
                    on_line(axis, d),
                ).start()

    def sum_terms(half):
        for axis in BOTH:
            for d in FAR:
                arrived(back_in.at[part(axis, d, half)], b_recv.at[axis, d, half])
        for i in reversed(range(half * PART, half * PART + PART)):
            for axis in (OTHER, OWN):
                d = SOURCES[axis][i]
                totals = [jnp.zeros((din, TILE), F32) for _ in BOTH]
                for e in (0,) + FAR:
                    value = back_in[line(axis, e) * PER + i].astype(F32) if e else own(axis, 0, i)
                    second = second_wanted(axis, e, i)
                    totals[0] += jnp.where(second, 0.0, value)
                    totals[1] += jnp.where(second, value, 0.0)
                for t in BOTH:
                    if d:
                        passed[d, t] = totals[t].astype(BF16)
                    else:
                        kept[t] = totals[t]
                if d:
                    there = OWN if d % 2 == 0 else OTHER
                    remote(
                        passed.at[d], landed.at[-d % R], sends.at[7], l_recv.at[-d % R], on_line(there, d)
                    ).start()

    def finish_backward():
        totals = [kept[t] for t in BOTH]
        for d in FAR:
            arrived(landed.at[d], l_recv.at[d])
            for t in BOTH:
                totals[t] += landed[d, t].astype(F32)
        for t in BOTH:
            grad_ref[:, t * TILE : (t + 1) * TILE] = totals[t].astype(BF16)

    grads, mixes = (0, gall, g_rows), (1, zall, x_rows)
    ask()
    z_start(*grads)
    spread()
    pass_on(0, FAR)
    z_pass(*grads, FAR[:3])
    pass_on(1, FAR)
    z_pass(*grads, FAR[3:])
    get_a.wait()
    get_slot.wait()
    z_finish(*grads)
    make_terms()
    send_terms(1)
    send_terms(0)
    w_start()
    have_all()
    aggregate()
    z_start(*mixes)
    w_forward()
    sum_terms(1)
    z_pass(*mixes, FAR)
    sum_terms(0)
    w_finish()
    z_finish(*mixes)
    finish_forward()
    finish_backward()

    for buf, n, k in (
        (gall, (2 * R - 1) * dout, 0),
        (zall, (2 * R - 1) * din, 1),
        (wall, (2 * R - 1) * din, 2),
        (asked, 2 * (R - 1) * 8, 3),
        (picked, 2 * (R - 1) * PER, 5),
        (sent, 2 * (R - 1) * PER, 6),
        (tiles, R - 1, 4),
        (passed, R - 1, 7),
    ):
        ref = buf.at[pl.ds(0, n)]
        remote(ref, ref, sends.at[k], w_recv.at[0], partner).wait_send()


def local(features, weight, tile_weights, tile_cols, tile_count, out_grad, relu_mask):
    din, dout = features.shape[1], out_grad.shape[1]
    rows = features.shape[0]
    vmem = pl.BlockSpec(memory_space=pltpu.VMEM)
    hbm = pl.BlockSpec(memory_space=pltpu.HBM)
    dma = pltpu.SemaphoreType.DMA
    act, grad = pl.pallas_call(
        kernel,
        out_shape=(
            pltpu.VMEM((dout, rows), BF16),
            pltpu.VMEM((din, rows), BF16),
        ),
        in_specs=[hbm] * 7,
        out_specs=(vmem, vmem),
        scratch_shapes=[
            pltpu.VMEM(weight.shape, BF16),
            pltpu.VMEM(tile_weights.shape, BF16),
            pltpu.VMEM((dout, rows), BF16),
            pltpu.VMEM((dout, rows), jnp.int32),
            pltpu.SMEM(tile_cols.shape, jnp.int32),
            pltpu.SMEM(tile_count.shape, jnp.int32),
            pltpu.VMEM((2, TILE), jnp.int32),
            pltpu.SMEM((2, TILE), jnp.int32),
            pltpu.VMEM((2 * R * 8, TILE), jnp.int32),
            pltpu.VMEM((2 * R * 8, TILE), jnp.int32),
            pltpu.VMEM((R, 2, din, TILE), BF16),
            pltpu.VMEM((LINES, din, TILE), BF16),
            pltpu.VMEM((LINES + 1, din, TILE), BF16),
            pltpu.VMEM((2 * (SLOTS + 1), din, TILE), F32),
            pltpu.VMEM((LINES, din, TILE), BF16),
            pltpu.VMEM((LINES, din, TILE), BF16),
            pltpu.VMEM((2, din, TILE), F32),
            pltpu.VMEM((R, 2, din, TILE), BF16),
            pltpu.VMEM((R, 2, din, TILE), BF16),
            pltpu.VMEM((2 * R * dout, rows), BF16),
            pltpu.VMEM((2 * R * din, rows), BF16),
            pltpu.VMEM((2 * R * din, 2 * dout), BF16),
            pltpu.VMEM((2 * dout, 2 * R * din), BF16),
            pltpu.VMEM((2 * dout, rows), F32),
            dma((8,)),
            dma((2, R)),
            dma((R,)),
            dma((2, R, 2)),
            dma((2, R, 2)),
            dma((R,)),
            dma((2, 2 * R)),
            dma((2 * R,)),
            dma((8,)),
        ],
        compiler_params=pltpu.CompilerParams(
            collective_id=0, has_side_effects=True, vmem_limit_bytes=60 * 1024 * 1024
        ),
        name="graph_layer",
    )(features.T, weight, tile_weights, tile_cols, tile_count, out_grad.T, relu_mask.T)
    return act.T, grad.T


def solution(mesh):
    in_specs = (
        P("node", "feat"),
        P("feat", None),
        P("node", None, None, None),
        P("node", None),
        P("node"),
        P("node", "feat"),
        P("node", "feat"),
    )
    out_specs = (P("node", "feat"), P("node", "feat"))
    return jax.shard_map(local, mesh=mesh, in_specs=in_specs, out_specs=out_specs, check_vma=False)
```

time: 201 us -> 52.4 us (0.26)
  waiting for transfers between devices: 93 us -> 0 us
  Pallas kernels: 0 us -> 49.9 us
  blocking collectives: 31 us -> 0 us
  starting transfers between devices: 25.5 us -> 0 us
  other arithmetic: 16 us -> 0 us
  local copies, waits for them, and re-layouts: 17.1 us -> 1.22 us
  between operations: 14.3 us -> 0.64 us
  matrix products: 3.64 us -> 0 us
    pallas_call x0 -> x1, Pallas kernels: none -> 49.9 us  [local(): pl.pallas_call(kernel, out_shape=(pltpu.VMEM((dout, rows), BF16), pltpu.V...]
    all_gather x1 -> x0, waiting for transfers between devices: 44 us -> none  [local(): everything = lax.all_gather(mixed_cols, 'node', axis=1, tiled=True)]
    reduce_scatter x1 -> x0, waiting for transfers between devices: 42.2 us -> none  [local(): lax.psum_scatter(lax.dot_general(weight_part, features, (((0,), (1,)), ((...]
    all_gather x1 -> x0, blocking collectives: 31 us -> none  [local(): lax.all_gather(back_cols, 'feat', axis=0, tiled=True)]
    all_to_all x2 -> x0, starting transfers between devices: 25.2 us -> none  [the longest x1 17.4 us: local(): lax.all_to_all(request_list, 'node', split_axis=0, concat_axis=0, tiled=T...]
    scatter-add x2 -> x0, other arithmetic: 12.5 us -> none  [the longest x1 10.5 us: local(): jax.ops.segment_sum(inbound_sums.reshape(count_blocks * CAP, cols_here *...]
    gather x2 -> x0, local copies, waits for them, and re-layouts: 8.53 us -> none  [local(): jnp.take(everything, node_index.reshape(-1), axis=1)]
    all_to_all x2 -> x0, waiting for transfers between devices: 6.79 us -> none  [the longest x1 4.9 us: local(): lax.all_to_all(request_list, 'node', split_axis=0, concat_axis=0, tiled=T...]
  transfers between devices with their start and end apart: 4 -> 0, of which waited for: 4 -> 0; matrix products, arithmetic and copies ran while one was open for 10% -> 0% of each run, Pallas kernels for 0% -> 0%
where the time goes in v2:
time: 52.4 us; the launch traced here: 51.8 us
  Pallas kernels  49.9 us (95%)
  local copies, waits for them, and re-layouts  1.22 us (2%)
  between operations  0.64 us (1%)
    pallas_call x1, Pallas kernels, local(): pl.pallas_call(kernel, out_shape=(pltpu.VMEM((dout, rows), BF16), pltpu.V...  49.9 us
    unnamed x2, local copies, waits for them, and re-layouts  1.22 us

profile of v2, /device:TPU:14, one launch (start us, length us, event | category | flops | bytes accessed | tf_op | source)
XLA Modules:
  0.0 51.8 jit_solution(16023682392767887936)
XLA Ops:
  0.6 49.9 %graph_layer.1 = (bf16[64,256]{1,0:T(8,128)(2,1)S(1)}, bf16[48,256]{1,0:T(8,128)(2,1)S(1)}) custom-call(bf16[48,256]{1,0:T(8,128)(2,1)} %bitcast.9, bf16[48,1024]{1,0:T(8,128)(2,1)} %w_hbm.1, bf16[2,8,128,128]{3,2,1,0:T(8,128)(2,1)} %a_hbm.1, s32[2,8]{1,0:T(2,128)} %cols_hbm.1, s32[2]{0:T(128)} %count_hbm.1, bf16[64,256]{1,0:T(8,128)(2,1)} %bitcast.8, ...), custom_call_target="tpu_custom_call" | custom-call | tf_op jit(solution)/shard_map/graph_layer/pallas_call | solution.py:344
  50.5 0.6 %copy.11 = bf16[256,64]{0,1:T(8,128)(2,1)} copy(bf16[256,64]{0,1:T(8,128)(2,1)S(1)} %bitcast.5) | data formatting | bytes 65536
  51.2 0.6 %copy.12 = bf16[256,48]{0,1:T(8,128)(2,1)} copy(bf16[256,48]{0,1:T(8,128)(2,1)S(1)} %bitcast.6) | data formatting | bytes 49152

commit v3 on v2

--- a/solution.py
+++ b/solution.py
@@ -176,7 +176,7 @@
                 ).start()
 
     def spread():
-        for d in FAR:
+        for d in NEAR:
             remote(tiles.at[0], tiles.at[-d % R], sends.at[4], s_recv.at[-d % R], on_line(OWN, d)).start()
 
     def second_wanted(axis, d, i):
@@ -296,12 +296,11 @@
 
     grads, mixes = (0, gall, g_rows), (1, zall, x_rows)
     ask()
+    spread()
     z_start(*grads)
-    spread()
     pass_on(0, FAR)
-    z_pass(*grads, FAR[:3])
     pass_on(1, FAR)
-    z_pass(*grads, FAR[3:])
+    z_pass(*grads, FAR)
     get_a.wait()
     get_slot.wait()
     z_finish(*grads)

time: 52.4 us -> 52.2 us (level)
  no operation moved by 1% of the time
where the time goes in v3:
time: 52.2 us; the launch traced here: 52.1 us
  Pallas kernels  50.2 us (96%)
  local copies, waits for them, and re-layouts  1.22 us (2%)
  between operations  0.64 us (1%)
    pallas_call x1, Pallas kernels, local(): pl.pallas_call(kernel, out_shape=(pltpu.VMEM((dout, rows), BF16), pltpu.V...  50.2 us
    unnamed x2, local copies, waits for them, and re-layouts  1.22 us

profile of v3, /device:TPU:14, one launch (start us, length us, event | category | flops | bytes accessed | tf_op | source)
XLA Modules:
  0.0 52.1 jit_solution(13825476368647055017)
XLA Ops:
  0.6 50.2 %graph_layer.1 = (bf16[64,256]{1,0:T(8,128)(2,1)S(1)}, bf16[48,256]{1,0:T(8,128)(2,1)S(1)}) custom-call(bf16[48,256]{1,0:T(8,128)(2,1)} %bitcast.9, bf16[48,1024]{1,0:T(8,128)(2,1)} %w_hbm.1, bf16[2,8,128,128]{3,2,1,0:T(8,128)(2,1)} %a_hbm.1, s32[2,8]{1,0:T(2,128)} %cols_hbm.1, s32[2]{0:T(128)} %count_hbm.1, bf16[64,256]{1,0:T(8,128)(2,1)} %bitcast.8, ...), custom_call_target="tpu_custom_call" | custom-call | tf_op jit(solution)/shard_map/graph_layer/pallas_call | solution.py:343
  50.8 0.6 %copy.11 = bf16[256,64]{0,1:T(8,128)(2,1)} copy(bf16[256,64]{0,1:T(8,128)(2,1)S(1)} %bitcast.5) | data formatting | bytes 65536
  51.5 0.6 %copy.12 = bf16[256,48]{0,1:T(8,128)(2,1)} copy(bf16[256,48]{0,1:T(8,128)(2,1)S(1)} %bitcast.6) | data formatting | bytes 49152
